TPU v7x, 32 devices: a whole 2x2x4 slice. The times are simulated.
32 devices in a mesh: ctx: 32 (over z, y, x, core).
Axes of the slice: x: 2, y: 2, z: 4, core: 2. Of those that a mesh axis runs over, the one named last changes fastest.
Arguments:
- tiles: bfloat16 [8192, 768], P('ctx'), may hold values from -6 to 6
- w_qkv: bfloat16 [768, 2304], replicated, may hold values from -1 to 1
- w_out: bfloat16 [768, 768], replicated, may hold values from -0.21875 to 0.21875
- cotangent: bfloat16 [8192, 768], P('ctx'), may hold values from -6 to 6
- offsets: int32 [2, 12], replicated, may hold values from 0 to 31, as said below
- pad_count: int32 [1], replicated, may hold values from 0 to 127
Outputs:
- out_rows: bfloat16 [8192, 768], P('ctx')
- grad_tiles: bfloat16 [8192, 768], P('ctx')
- grad_wqkv: float32 [768, 2304], P('ctx')
- grad_wout: float32 [768, 768], P('ctx')
Inputs may be any that keep to these rules, and one draw needn't show every extreme that they name: offsets[0, h] is below 8; offsets[1, h] is below 32.
All inputs are finite; a program needn't handle non-finite values.
Results may differ from a plain program's by a relative error of at most 0.033.
Values may be sent and summed in bfloat16 or wider, within the bound.
No kernel may reach another device: no remote copies, remote signals or barrier semaphores. Data moves between devices by JAX's collectives and lax.ppermute only.
A program may use at most 128 MiB of HBM per device.

v0:
```python
import jax
import jax.numpy as jnp
from jax import lax
from jax.sharding import PartitionSpec as P

D = 768
HEADS = 12
HEAD_DIM = 64
GROUP = 8
scale_factor = 0.125
block_rows = 512


def from_partner(value, axis, apart):
    mask = 2**apart
    pairs = [(source, source ^ mask) for source in range(lax.axis_size(axis))]
    return lax.ppermute(value, axis, pairs)


def pick_rows(array_in, stride, offsets_row):
    row_count = array_in.shape[0]
    blocked = array_in.reshape((row_count // stride, stride) + array_in.shape[1:])
    chosen = jnp.arange(stride, dtype=jnp.int32)[:, None] == offsets_row[None, :]
    chosen = chosen.reshape((1, stride, offsets_row.shape[0]) + (1,) * (array_in.ndim - 2))
    return jnp.sum(jnp.where(chosen, blocked, jnp.zeros((), array_in.dtype)), axis=1)


def spread_rows(array_in, stride, offsets_row, fill):
    chosen = jnp.arange(stride, dtype=jnp.int32)[:, None] == offsets_row[None, :]
    chosen = chosen.reshape((1, stride, offsets_row.shape[0]) + (1,) * (array_in.ndim - 2))
    widened = jnp.where(chosen, array_in[:, None], jnp.asarray(fill, array_in.dtype))
    return widened.reshape((array_in.shape[0] * stride,) + array_in.shape[1:])


def masked_scores(queries, key_rows, key_valid):
    scores = (
        jnp.einsum("nhe,mhe->hnm", queries, key_rows, preferred_element_type=jnp.float32)
        * scale_factor
    )
    return jnp.where(key_valid[:, None, :], scores, -jnp.inf)


def level_forward(queries, key_rows, value_rows, key_valid):
    scores = masked_scores(queries, key_rows, key_valid)
    peak = jnp.max(scores, axis=-1, keepdims=True)
    log_total = peak[..., 0] + jnp.log(jnp.sum(jnp.exp(scores - peak), axis=-1))
    weights = jnp.exp(scores - log_total[..., None]).astype(jnp.bfloat16)
    mixed = jnp.einsum("hnm,mhe->nhe", weights, value_rows, preferred_element_type=jnp.float32)
    return (mixed, log_total.T)


def level_grads(
    queries,
    key_rows,
    value_rows,
    key_valid,
    log_total,
    grad_out,
    delta_rows,
    want_queries,
    want_keys,
):
    scores = masked_scores(queries, key_rows, key_valid)
    probs = jnp.exp(scores - log_total.T[:, :, None])
    grad_probs = jnp.einsum(
        "nhe,mhe->hnm", grad_out, value_rows, preferred_element_type=jnp.float32
    )
    grad_scores = (probs * (grad_probs - delta_rows.T[:, :, None])).astype(jnp.bfloat16)
    results = []
    if want_queries:
        results.append(
            scale_factor
            * jnp.einsum("hnm,mhe->nhe", grad_scores, key_rows, preferred_element_type=jnp.float32)
        )
    if want_keys:
        results.append(
            scale_factor
            * jnp.einsum("hnm,nhe->mhe", grad_scores, queries, preferred_element_type=jnp.float32)
        )
        results.append(
            jnp.einsum(
                "hnm,nhe->mhe",
                probs.astype(jnp.bfloat16),
                grad_out,
                preferred_element_type=jnp.float32,
            )
        )
    return tuple(results)


def forward_blocks(queries, key_rows, value_rows, key_valid):
    count = queries.shape[0]
    size = min(count, block_rows)
    return level_forward(queries, key_rows, value_rows, key_valid)


def grads_blocks(queries, key_rows, value_rows, key_valid, log_total, grad_out, delta_rows):
    count = queries.shape[0]
    size = min(count, block_rows)
    return level_grads(
        queries, key_rows, value_rows, key_valid, log_total, grad_out, delta_rows, True, True
    )


def per_device(tiles, w_qkv, w_out, cotangent, offsets, pad_count):
    row_count = tiles.shape[0]
    dev_count = lax.axis_size("ctx")
    own_index = lax.axis_index("ctx")
    shaped = (row_count, HEADS, HEAD_DIM)
    packed = jnp.dot(tiles, w_qkv, preferred_element_type=jnp.float32).astype(jnp.bfloat16)
    queries = packed[:, :D].reshape(shaped)
    key_all = packed[:, D : 2 * D].reshape(shaped)
    value_all = packed[:, 2 * D :].reshape(shaped)
    limit = row_count * dev_count - pad_count[0]
    base_pos = own_index * row_count + jnp.arange(row_count, dtype=jnp.int32)
    valid_near = jnp.broadcast_to((base_pos < limit)[None, :], (HEADS, row_count))
    mixed_near, lse_near = forward_blocks(queries, key_all, value_all, valid_near)
    offs_mid = offsets[0]
    mid_rows = row_count // GROUP
    query_mid = pick_rows(queries, GROUP, offs_mid)
    key_mid = pick_rows(key_all, GROUP, offs_mid)
    value_mid = pick_rows(value_all, GROUP, offs_mid)
    gathered = jnp.stack([key_mid.reshape(mid_rows, D), value_mid.reshape(mid_rows, D)])
    bit_total = GROUP.bit_length() - 1
    for bit_index in range(bit_total):
        partner = from_partner(gathered, "ctx", bit_index)
        upper = own_index // 2**bit_index % 2 == 1
        gathered = jnp.where(
            upper,
            jnp.concatenate([partner, gathered], axis=1),
            jnp.concatenate([gathered, partner], axis=1),
        )
    keys_group = gathered[0].reshape(shaped)
    values_group = gathered[1].reshape(shaped)
    group_start = own_index // GROUP * GROUP * row_count
    mid_pos = (
        group_start + jnp.arange(row_count, dtype=jnp.int32)[:, None] * GROUP + offs_mid[None, :]
    )
    valid_mid = (mid_pos < limit).T
    mixed_mid, lse_mid = level_forward(query_mid, keys_group, values_group, valid_mid)
    offs_far = offsets[1]
    far_rows = row_count // dev_count
    query_far = pick_rows(queries, dev_count, offs_far)
    key_far = pick_rows(key_all, dev_count, offs_far)
    value_far = pick_rows(value_all, dev_count, offs_far)
    far_all = lax.all_gather(
        jnp.stack([key_far.reshape(far_rows, D), value_far.reshape(far_rows, D)]),
        "ctx",
        axis=1,
        tiled=True,
    )
    keys_far_all = far_all[0].reshape(shaped)
    values_far_all = far_all[1].reshape(shaped)
    far_pos = jnp.arange(row_count, dtype=jnp.int32)[:, None] * dev_count + offs_far[None, :]
    valid_far = (far_pos < limit).T
    mixed_far, lse_far = level_forward(query_far, keys_far_all, values_far_all, valid_far)
    lse_mid_all = spread_rows(lse_mid, GROUP, offs_mid, -jnp.inf)
    lse_far_all = spread_rows(lse_far, dev_count, offs_far, -jnp.inf)
    log_total = jnp.logaddexp(jnp.logaddexp(lse_near, lse_mid_all), lse_far_all)
    combined = jnp.exp(lse_near - log_total)[..., None] * mixed_near
    combined = combined + jnp.exp(lse_mid_all - log_total)[..., None] * spread_rows(
        mixed_mid, GROUP, offs_mid, 0.0
    )
    combined = combined + jnp.exp(lse_far_all - log_total)[..., None] * spread_rows(
        mixed_far, dev_count, offs_far, 0.0
    )
    attn = combined.astype(jnp.bfloat16).reshape(row_count, D)
    out_rows = (
        tiles.astype(jnp.float32) + jnp.dot(attn, w_out, preferred_element_type=jnp.float32)
    ).astype(jnp.bfloat16)
    grad_attn = jnp.dot(cotangent, w_out.T, preferred_element_type=jnp.float32).astype(jnp.bfloat16)
    grad_wout_part = lax.dot_general(
        attn, cotangent, (((0,), (0,)), ((), ())), preferred_element_type=jnp.float32
    )
    grad_heads = grad_attn.reshape(shaped)
    delta_rows = jnp.sum(
        grad_heads.astype(jnp.float32) * attn.reshape(shaped).astype(jnp.float32), axis=-1
    )
    grad_query_near, grad_key_near, grad_value_near = grads_blocks(
        queries, key_all, value_all, valid_near, log_total, grad_heads, delta_rows
    )
    lse_mid_rows = pick_rows(log_total, GROUP, offs_mid)
    grad_mid_rows = pick_rows(grad_heads, GROUP, offs_mid)
    delta_mid_rows = pick_rows(delta_rows, GROUP, offs_mid)
    grad_query_mid, grad_key_group, grad_value_group = level_grads(
        query_mid,
        keys_group,
        values_group,
        valid_mid,
        lse_mid_rows,
        grad_mid_rows,
        delta_mid_rows,
        True,
        True,
    )
    summed = jnp.stack(
        [grad_key_group.reshape(row_count, D), grad_value_group.reshape(row_count, D)]
    )
    for bit_index in reversed(range(bit_total)):
        half = summed.shape[1] // 2
        lower = summed[:, :half]
        higher = summed[:, half:]
        upper = own_index // 2**bit_index % 2 == 1
        outgoing = jnp.where(upper, lower, higher)
        summed = jnp.where(upper, higher, lower) + from_partner(outgoing, "ctx", bit_index)
    grad_key_mid = summed[0].reshape(mid_rows, HEADS, HEAD_DIM)
    grad_value_mid = summed[1].reshape(mid_rows, HEADS, HEAD_DIM)
    lse_far_rows = pick_rows(log_total, dev_count, offs_far)
    grad_far_rows = pick_rows(grad_heads, dev_count, offs_far)
    delta_far_rows = pick_rows(delta_rows, dev_count, offs_far)
    row_block = jnp.stack(
        [query_far.reshape(far_rows, D), grad_far_rows.reshape(far_rows, D)]
    ).astype(jnp.float32)
    stat_block = jnp.stack([lse_far_rows, delta_far_rows])
    rows_all, stats_all = (
        lax.all_gather(row_block, "ctx", axis=1, tiled=True),
        lax.all_gather(stat_block, "ctx", axis=1, tiled=True),
    )
    query_all = rows_all[0].astype(jnp.bfloat16).reshape(shaped)
    grad_all = rows_all[1].astype(jnp.bfloat16).reshape(shaped)
    (grad_query_far,) = level_grads(
        query_far,
        keys_far_all,
        values_far_all,
        valid_far,
        lse_far_rows,
        grad_far_rows,
        delta_far_rows,
        True,
        False,
    )
    own_pos = (own_index * far_rows + jnp.arange(far_rows, dtype=jnp.int32))[
        :, None
    ] * dev_count + offs_far[None, :]
    grad_key_far, grad_value_far = level_grads(
        query_all,
        key_far,
        value_far,
        (own_pos < limit).T,
        stats_all[0],
        grad_all,
        stats_all[1],
        False,
        True,
    )
    grad_query = (
        grad_query_near
        + spread_rows(grad_query_mid, GROUP, offs_mid, 0.0)
        + spread_rows(grad_query_far, dev_count, offs_far, 0.0)
    )
    grad_key = (
        grad_key_near
        + spread_rows(grad_key_mid, GROUP, offs_mid, 0.0)
        + spread_rows(grad_key_far, dev_count, offs_far, 0.0)
    )
    grad_value = (
        grad_value_near
        + spread_rows(grad_value_mid, GROUP, offs_mid, 0.0)
        + spread_rows(grad_value_far, dev_count, offs_far, 0.0)
    )
    grad_packed = jnp.concatenate(
        [
            grad_query.reshape(row_count, D),
            grad_key.reshape(row_count, D),
            grad_value.reshape(row_count, D),
        ],
        axis=1,
    ).astype(jnp.bfloat16)
    grad_tiles = jnp.dot(grad_packed, w_qkv.T, preferred_element_type=jnp.float32).astype(
        jnp.bfloat16
    )
    grad_wqkv_part = lax.dot_general(
        tiles, grad_packed, (((0,), (0,)), ((), ())), preferred_element_type=jnp.float32
    )
    grad_wqkv, grad_wout = (
        lax.psum_scatter(grad_wqkv_part, "ctx", scatter_dimension=0, tiled=True),
        lax.psum_scatter(grad_wout_part, "ctx", scatter_dimension=0, tiled=True),
    )
    return (out_rows, grad_tiles, grad_wqkv, grad_wout)


def solution(mesh):
    return jax.shard_map(
        per_device,
        mesh=mesh,
        in_specs=(P("ctx", None), P(), P(), P("ctx", None), P(), P()),
        out_specs=(P("ctx", None), P("ctx", None), P("ctx", None), P("ctx", None)),
        check_vma=False,
    )
```

profile of v0, /device:TPU:0, one launch (start us, length us, event | category | flops | bytes accessed | tf_op | source)
XLA Modules:
  0.0 557.5 jit_solution(5915493366938448926)
XLA Ops:
  8.1 2.8 convolution_convert_fusion.2
  16.5 2.5 reshape_reshape.25
  19.0 2.4 reshape_reshape.26
  21.4 2.4 reshape_reshape.24
  23.8 4.6 select_reduce_fusion.1
  41.9 2.5 reshape_reshape.28
  44.4 2.4 reshape_reshape.29
  46.9 2.4 reshape_reshape.27
  50.6 4.1 select_reduce_fusion
  60.6 45.0 %all_gather.10 = bf16[2,256,768]{2,1,0:T(8,128)(2,1)S(1)} all-gather(bf16[2,8,768]{2,1,0:T(8,128)(2,1)S(1)} %maximum_convert_fusion), channel_id=1, replica_groups=mesh['ctx'=32] {'ctx'}, dimensions={1}, use_global_device_ids=true | all-gather | bytes 811008 | tf_op jit(solution)/shard_map/all_gather | solution.py:216
  106.6 39.1 %all_gather.9 = bf16[2,256,768]{2,1,0:T(8,128)(2,1)S(1)} all-gather(bf16[2,8,768]{2,1,0:T(8,128)(2,1)S(1)} %pad_maximum_fusion.4), channel_id=1, replica_groups=mesh['ctx'=32] {'ctx'}, dimensions={1}, use_global_device_ids=true | all-gather | bytes 811008 | tf_op jit(solution)/shard_map/all_gather | solution.py:146
  151.3 3.5 fusion.85
  183.6 2.8 copy.156
  189.1 2.9 exponential_reduce_fusion
  192.0 6.8 %collective-permute-done.2 = bf16[2,128,768]{2,1,0:T(8,128)(2,1)S(1)} collective-permute-done((bf16[2,128,768]{2,1,0:T(8,128)(2,1)S(1)}, bf16[2,128,768]{2,1,0:T(8,128)(2,1)S(1)}, u32[]{:S(2)}, u32[]{:S(2)}) %collective-permute-start.2) | collective-permute-done | bytes 393248 | tf_op jit(solution)/shard_map/ppermute | solution.py:17
  215.5 2.8 copy.154
  218.2 4.7 multiply_reduce_fusion
  238.4 37.4 %all_gather.11 = f32[2,256,12]{2,1,0:T(8,128)S(1)} all-gather(f32[2,8,12]{2,1,0:T(8,128)S(1)} %pad_maximum_fusion.5), channel_id=1, replica_groups=mesh['ctx'=32] {'ctx'}, dimensions={1}, use_global_device_ids=true | all-gather | bytes 25344 | tf_op jit(solution)/shard_map/all_gather | solution.py:217
  297.1 9.6 %collective-permute-done.3 = f32[2,128,768]{2,1,0:T(8,128)} collective-permute-done((f32[2,128,768]{2,1,0:T(8,128)}, f32[2,128,768]{2,1,0:T(8,128)}, u32[]{:S(2)}, u32[]{:S(2)}) %collective-permute-start.3) | collective-permute-done | bytes 786464 | tf_op jit(solution)/shard_map/ppermute | solution.py:17
  312.5 2.8 copy.161
  317.3 2.7 copy.183
  322.1 2.7 copy.179
  326.9 2.8 copy.163
  330.0 3.1 multiply_convert_fusion
  344.6 2.9 copy.182
  349.7 2.8 copy.170
  352.6 2.8 fusion.30
  358.7 4.0 convolution_bitcast_fusion
  362.7 8.0 %copy.190 = f32[768,2304]{1,0:T(8,128)} copy(f32[768,2304]{0,1:T(8,128)} %convolution_bitcast_fusion) | data formatting | bytes 14155776
  370.8 2.8 fusion.25
  375.6 49.7 %reduce-scatter.5.cloned.1.call-done = f32[24,768]{1,0:T(8,128)} async-done(((f32[768,768]{1,0:T(8,128)}), f32[24,768]{1,0:T(8,128)}) %reduce-scatter.5.cloned.1.call-update) | async-done | bytes 73744 | tf_op jit(solution)/shard_map/reduce_scatter | solution.py:277
  425.2 125.5 %reduce-scatter.7.cloned.1.call-done = f32[24,2304]{1,0:T(8,128)} async-done(((f32[768,2304]{1,0:T(8,128)}), f32[24,2304]{1,0:T(8,128)}) %reduce-scatter.7.cloned.1.call-update) | async-done | bytes 221200
  (198 shorter events, 149.0 us)
Async XLA Ops:
  7.2 6.2 %copy-start = (bf16[768,2304]{1,0:T(8,128)(2,1)S(1)}, bf16[768,2304]{1,0:T(8,128)(2,1)}, u32[]{:S(2)}) copy-start(bf16[768,2304]{1,0:T(8,128)(2,1)} %param.7) | copy-start | bytes 10616836
  7.2 418.0 %reduce-scatter.5.cloned.1.call-start = ((), (), s32[]{:S(2)}) async-start(), calls=%async_computation.2 | async-start | bytes 2433024 | tf_op jit(solution)/shard_map/reduce_scatter | solution.py:277
  8.1 5.3 copy-start.36
  8.1 140.5 %copy-start.34 = (s32[12]{0:T(128)}, s32[12]{0:T(128)S(1)}, u32[]{:S(2)}) copy-start(s32[12]{0:T(128)S(1)} %get-tuple-element.55) | copy-start | bytes 148
  8.1 15.8 %copy-start.35 = (pred[8,12]{1,0:T(8,128)(4,1)}, pred[8,12]{1,0:T(8,128)(4,1)S(1)}, u32[]{:S(2)}) copy-start(pred[8,12]{1,0:T(8,128)(4,1)S(1)} %iota_compare_fusion.1) | copy-start | bytes 292
  34.6 122.8 %collective-permute-start = (bf16[2,32,768]{2,1,0:T(8,128)(2,1)}, bf16[2,32,768]{2,1,0:T(8,128)(2,1)}, u32[]{:S(2)}, u32[]{:S(2)}) collective-permute-start(bf16[2,32,768]{2,1,0:T(8,128)(2,1)} %constant_dynamic-update-slice_fusion), channel_id=1, source_target_pairs={{0,1},{1,0},{2,3},{3,2},{4,5},{5,4},{6,7},{7,6},{8,9},{9,8},{10,11... | collective-permute-start | bytes 294920 | tf_op jit(solution)/shard_map/ppermute | solution.py:17
  50.6 4.2 copy-start.32
  59.9 46.7 %copy-start.31 = (bf16[1,8,768]{2,1,0:T(8,128)(2,1)S(1)}, bf16[1,8,768]{2,1,0:T(8,128)(2,1)}, u32[]{:S(2)}) copy-start(bf16[1,8,768]{2,1,0:T(8,128)(2,1)} %stack_reshape.27) | copy-start | bytes 36868
  106.6 42.0 %copy-start.37 = (s32[12]{0:T(128)S(1)}, s32[12]{0:T(128)}, u32[]{:S(2)}) copy-start(s32[12]{0:T(128)} %copy-done.36) | copy-start | bytes 148
  106.6 42.0 %copy-start.38 = (s32[256]{0:T(256)S(1)}, s32[256]{0:T(256)}, u32[]{:S(2)}) copy-start(s32[256]{0:T(256)} %iota_multiply_fusion) | copy-start | bytes 3076
  106.6 42.0 %copy-start.39 = (s32[256]{0:T(256)S(1)}, s32[256]{0:T(256)}, u32[]{:S(2)}) copy-start(s32[256]{0:T(256)} %multiply_add_fusion) | copy-start | bytes 3076
  154.8 34.2 %copy-start.29 = (f32[12,256]{1,0:T(8,128)}, f32[12,256]{1,0:T(8,128)S(1)}, u32[]{:S(2)}) copy-start(f32[12,256]{1,0:T(8,128)S(1)} %get-tuple-element.60) | copy-start | bytes 36868
  159.1 27.2 %collective-permute-start.1 = (bf16[2,64,768]{2,1,0:T(8,128)(2,1)}, bf16[2,64,768]{2,1,0:T(8,128)(2,1)}, u32[]{:S(2)}, u32[]{:S(2)}) collective-permute-start(bf16[2,64,768]{2,1,0:T(8,128)(2,1)} %maximum_select_fusion.2), channel_id=1, source_target_pairs={{0,2},{1,3},{2,0},{3,1},{4,6},{5,7},{6,4},{7,5},{8,10},{9,11},{10,... | collective-permute-start | bytes 589832 | tf_op jit(solution)/shard_map/ppermute | solution.py:17
  187.7 11.1 %collective-permute-start.2 = (bf16[2,128,768]{2,1,0:T(8,128)(2,1)S(1)}, bf16[2,128,768]{2,1,0:T(8,128)(2,1)S(1)}, u32[]{:S(2)}, u32[]{:S(2)}) collective-permute-start(bf16[2,128,768]{2,1,0:T(8,128)(2,1)S(1)} %maximum_select_fusion.1), channel_id=1, source_target_pairs={{0,4},{1,5},{2,6},{3,7},{4,0},{5,1},{6,2},{7,3},{8,12},{9,13},{10,... | collective-permute-start | bytes 1179656 | tf_op jit(solution)/shard_map/ppermute | solution.py:17
  199.1 2.9 copy-start.33
  230.9 3.6 copy-start.4
  230.9 3.6 copy-start.9
  230.9 3.6 copy-start.23
  286.5 20.1 %collective-permute-start.3 = (f32[2,128,768]{2,1,0:T(8,128)}, f32[2,128,768]{2,1,0:T(8,128)}, u32[]{:S(2)}, u32[]{:S(2)}) collective-permute-start(f32[2,128,768]{2,1,0:T(8,128)} %broadcast_select_fusion), channel_id=1, source_target_pairs={{0,4},{1,5},{2,6},{3,7},{4,0},{5,1},{6,2},{7,3},{8,12},{9,13},{10,... | collective-permute-start | bytes 2359304 | tf_op jit(solution)/shard_map/ppermute | solution.py:17
  297.1 14.6 %copy-start.8 = (bf16[1,256,768]{1,2,0:T(8,128)(2,1)S(1)}, bf16[1,256,768]{1,2,0:T(8,128)(2,1)}, u32[]{:S(2)}) copy-start(bf16[1,256,768]{1,2,0:T(8,128)(2,1)} %copy.176) | copy-start | bytes 1179652
  297.1 14.6 %copy-start.22 = (f32[12,256,8]{1,2,0:T(8,128)S(1)}, f32[12,256,8]{1,2,0:T(8,128)}, u32[]{:S(2)}) copy-start(f32[12,256,8]{1,2,0:T(8,128)} %fusion.41) | copy-start | bytes 294916
  310.1 23.1 %collective-permute-start.4 = (f32[2,64,768]{2,1,0:T(8,128)}, f32[2,64,768]{2,1,0:T(8,128)}, u32[]{:S(2)}, u32[]{:S(2)}) collective-permute-start(f32[2,64,768]{2,1,0:T(8,128)} %slice_select_fusion), channel_id=1, source_target_pairs={{0,2},{1,3},{2,0},{3,1},{4,6},{5,7},{6,4},{7,5},{8,10},{9,11},{10,... | collective-permute-start | bytes 1179656 | tf_op jit(solution)/shard_map/ppermute | solution.py:17
  329.8 220.9 %reduce-scatter.7.cloned.1.call-start = ((), (), s32[]{:S(2)}) async-start(), calls=%async_computation.3 | async-start | bytes 7299072
  330.0 3.1 copy-start.6
  333.1 3.4 copy-start.2
  334.9 1.6 collective-permute-start.5
  352.5 3.1 copy-start.1
  352.6 3.1 copy-start.7
  352.6 3.1 copy-start.26
  352.6 3.1 copy-start.28
  355.7 3.0 copy-start.14
  355.7 3.0 copy-start.24
  (16 other events, 30.0 us)
Sparse Core Ops, SparseCore 0:
  329.9 95.2 reduce-scatter.4
  432.4 118.2 reduce-scatter.6
where the time goes:
time: 561 us; the launch traced here: 558 us
  waiting for transfers between devices  192 us (34%)
  local copies, waits for them, and re-layouts  140 us (25%)
  blocking collectives  121 us (22%)
  matrix products  52.5 us (9%)
  other arithmetic  32.9 us (6%)
  between operations  15.1 us (3%)
    unnamed x3, waiting for transfers between devices  126 us
    broadcast_in_dim x28, local copies, waits for them, and re-layouts, spread_rows(): jnp.where(chosen, array_in[:, None], jnp.asarray(fill, array_in.dtype))  53.5 us
    reduce_scatter x1, waiting for transfers between devices, per_device(): lax.psum_scatter(grad_wout_part, 'ctx', scatter_dimension=0, tiled=True)  49.7 us
    all_gather x1, blocking collectives, per_device(): lax.all_gather(row_block, 'ctx', axis=1, tiled=True)  45 us
    all_gather x1, blocking collectives, per_device(): lax.all_gather(jnp.stack([key_far.reshape(far_rows, D), value_far.reshape...  39.1 us
    all_gather x1, blocking collectives, per_device(): lax.all_gather(stat_block, 'ctx', axis=1, tiled=True)  37.4 us
    another operation x8, local copies, waits for them, and re-layouts, pick_rows(): array_in.reshape((row_count // stride, stride) + array_in.shape[1:])  19.6 us
    ppermute x6, waiting for transfers between devices, from_partner(): return lax.ppermute(value, axis, pairs)  16.4 us
  transfers between devices with their start and end apart: 8, of which 4 were waited for; matrix products, arithmetic and copies ran while one was open for 25% of the time, Pallas kernels for 0%

commit v1 on v0

--- a/solution.py
+++ b/solution.py
@@ -9,6 +9,28 @@
 GROUP = 8
 scale_factor = 0.125
 block_rows = 512
+
+
+def laid_out(parts, dim):
+    parts = jnp.moveaxis(parts, 0, dim)
+    dims = parts.shape
+    return parts.reshape(*dims[:dim], dims[dim] * dims[dim + 1], *dims[dim + 2 :])
+
+
+def grow_blocks(array, axis):
+    size = lax.axis_size(axis)
+    pieces = array[None]
+    for level in range(size.bit_length() - 1):
+        distance = 1 << level
+        other = lax.ppermute(pieces, axis, [(i, i ^ distance) for i in range(size)])
+        both = jnp.stack([pieces, other])
+        upper = lax.axis_index(axis) >> level & 1
+        pieces = jnp.where(upper == 0, both, both[::-1]).reshape(-1, *array.shape)
+    return pieces
+
+
+def collect(x, axis, dim):
+    return laid_out(grow_blocks(x, axis), dim)
 
 
 def from_partner(value, axis, apart):
@@ -143,11 +165,8 @@
     query_far = pick_rows(queries, dev_count, offs_far)
     key_far = pick_rows(key_all, dev_count, offs_far)
     value_far = pick_rows(value_all, dev_count, offs_far)
-    far_all = lax.all_gather(
-        jnp.stack([key_far.reshape(far_rows, D), value_far.reshape(far_rows, D)]),
-        "ctx",
-        axis=1,
-        tiled=True,
+    far_all = collect(
+        jnp.stack([key_far.reshape(far_rows, D), value_far.reshape(far_rows, D)]), "ctx", 1
     )
     keys_far_all = far_all[0].reshape(shaped)
     values_far_all = far_all[1].reshape(shaped)

time: 561 us -> 530 us (0.945)
  blocking collectives: 121 us -> 84.6 us
    all_gather x1 -> x0, blocking collectives: 39.1 us -> none  [per_device(): lax.all_gather(jnp.stack([key_far.reshape(far_rows, D), value_far.reshape...]
    another operation x0 -> x4, local copies, waits for them, and re-layouts: none -> 10 us  [the longest x2 5.03 us: per_device(): keys_far_all = far_all[0].reshape(shaped)]
    ppermute x0 -> x5, waiting for transfers between devices: none -> 7.62 us  [grow_blocks(): other = lax.ppermute(pieces, axis, [(i, i ^ distance) for i in range(size)])]
    unnamed x82 -> x95, local copies, waits for them, and re-layouts: 13.9 us -> 15 us
  transfers between devices with their start and end apart: 8 -> 13, of which waited for: 4 -> 6; matrix products, arithmetic and copies ran while one was open for 25% -> 27% of each run, Pallas kernels for 0% -> 0%
where the time goes in v1:
time: 530 us; the launch traced here: 527 us
  waiting for transfers between devices  196 us (37%)
  local copies, waits for them, and re-layouts  144 us (27%)
  blocking collectives  84.6 us (16%)
  matrix products  48.5 us (9%)
  other arithmetic  35.7 us (7%)
  between operations  15.3 us (3%)
    unnamed x3, waiting for transfers between devices  125 us
    reduce_scatter x1, waiting for transfers between devices, per_device(): lax.psum_scatter(grad_wout_part, 'ctx', scatter_dimension=0, tiled=True)  51.3 us
    broadcast_in_dim x28, local copies, waits for them, and re-layouts, spread_rows(): jnp.where(chosen, array_in[:, None], jnp.asarray(fill, array_in.dtype))  51 us
    all_gather x1, blocking collectives, per_device(): lax.all_gather(row_block, 'ctx', axis=1, tiled=True)  45.5 us
    all_gather x1, blocking collectives, per_device(): lax.all_gather(stat_block, 'ctx', axis=1, tiled=True)  39.1 us
    another operation x8, local copies, waits for them, and re-layouts, pick_rows(): array_in.reshape((row_count // stride, stride) + array_in.shape[1:])  19.5 us
    unnamed x95, local copies, waits for them, and re-layouts  15 us
    reduce_sum x4, other arithmetic, pick_rows(): jnp.sum(jnp.where(chosen, blocked, jnp.zeros((), array_in.dtype)), axis=1)  11.6 us
  transfers between devices with their start and end apart: 13, of which 6 were waited for; matrix products, arithmetic and copies ran while one was open for 27% of the time, Pallas kernels for 0%

profile of v1, /device:TPU:0, one launch (start us, length us, event | category | flops | bytes accessed | tf_op | source)
XLA Modules:
  0.0 526.6 jit_solution(13658230121975541549)
XLA Ops:
  9.2 2.6 convolution_convert_fusion.2
  17.4 2.4 reshape_reshape.28
  22.2 2.4 reshape_reshape.27
  24.7 4.1 select_reduce_fusion
  34.6 2.4 reshape_reshape.25
  39.5 2.4 reshape_reshape.24
  41.9 4.6 select_reduce_fusion.1
  61.5 45.5 %all_gather.6 = bf16[2,256,768]{2,1,0:T(8,128)(2,1)S(1)} all-gather(bf16[2,8,768]{2,1,0:T(8,128)(2,1)S(1)} %maximum_convert_fusion), channel_id=1, replica_groups=mesh['ctx'=32] {'ctx'}, dimensions={1}, use_global_device_ids=true | all-gather | bytes 811008 | tf_op jit(solution)/shard_map/all_gather | solution.py:235
  112.6 4.4 collective-permute-done.4
  119.2 3.3 collective-permute-done.5
  157.0 2.8 copy.169
  162.0 2.4 reshape_squeeze.13
  164.5 2.6 copy.165
  175.4 2.4 reshape_squeeze.15
  177.8 2.6 copy.170
  183.0 2.8 copy.171
  185.8 4.7 multiply_reduce_fusion
  205.9 39.1 %all_gather.7 = f32[2,256,12]{2,1,0:T(8,128)S(1)} all-gather(f32[2,8,12]{2,1,0:T(8,128)S(1)} %pad_maximum_fusion.9), channel_id=1, replica_groups=mesh['ctx'=32] {'ctx'}, dimensions={1}, use_global_device_ids=true | all-gather | bytes 25344 | tf_op jit(solution)/shard_map/all_gather | solution.py:236
  266.3 9.5 %collective-permute-done.8 = f32[2,128,768]{2,1,0:T(8,128)} collective-permute-done((f32[2,128,768]{2,1,0:T(8,128)}, f32[2,128,768]{2,1,0:T(8,128)}, u32[]{:S(2)}, u32[]{:S(2)}) %collective-permute-start.8) | collective-permute-done | bytes 786464 | tf_op jit(solution)/shard_map/ppermute | solution.py:39
  280.3 2.8 copy.176
  285.1 2.8 copy.200
  289.9 2.7 copy.196
  294.7 2.8 copy.180
  297.6 3.0 multiply_convert_fusion
  312.1 2.8 copy.199
  317.2 2.8 copy.187
  320.0 2.8 fusion.30
  326.2 4.0 convolution_bitcast_fusion
  330.2 8.1 %copy.207 = f32[768,2304]{1,0:T(8,128)} copy(f32[768,2304]{0,1:T(8,128)} %convolution_bitcast_fusion) | data formatting | bytes 14155776
  338.3 2.8 fusion.25
  343.1 51.3 %reduce-scatter.5.cloned.1.call-done = f32[24,768]{1,0:T(8,128)} async-done(((f32[768,768]{1,0:T(8,128)}), f32[24,768]{1,0:T(8,128)}) %reduce-scatter.5.cloned.1.call-update) | async-done | bytes 73744 | tf_op jit(solution)/shard_map/reduce_scatter | solution.py:296
  394.4 125.4 %reduce-scatter.7.cloned.1.call-done = f32[24,2304]{1,0:T(8,128)} async-done(((f32[768,2304]{1,0:T(8,128)}), f32[24,2304]{1,0:T(8,128)}) %reduce-scatter.7.cloned.1.call-update) | async-done | bytes 221200
  (233 shorter events, 154.0 us)
Async XLA Ops:
  7.2 7.1 %copy-start = (bf16[768,2304]{1,0:T(8,128)(2,1)S(1)}, bf16[768,2304]{1,0:T(8,128)(2,1)}, u32[]{:S(2)}) copy-start(bf16[768,2304]{1,0:T(8,128)(2,1)} %param.7) | copy-start | bytes 10616836
  7.2 387.2 %reduce-scatter.5.cloned.1.call-start = ((), (), s32[]{:S(2)}) async-start(), calls=%async_computation.2 | async-start | bytes 2433024 | tf_op jit(solution)/shard_map/reduce_scatter | solution.py:296
  31.7 79.4 %collective-permute-start.3 = (bf16[1,2,8,768]{3,2,1,0:T(8,128)(2,1)}, bf16[1,2,8,768]{3,2,1,0:T(8,128)(2,1)}, u32[]{:S(2)}, u32[]{:S(2)}) collective-permute-start(bf16[1,2,8,768]{3,2,1,0:T(8,128)(2,1)} %bitcast.238), channel_id=1, source_target_pairs={{0,1},{1,0},{2,3},{3,2},{4,5},{5,4},{6,7},{7,6},{8,9},{9,8},{10,11... | collective-permute-start | bytes 73736 | tf_op jit(solution)/shard_map/ppermute | solution.py:25
  37.0 4.9 copy-start.42
  41.9 4.7 copy-start.40
  52.7 65.2 %collective-permute-start = (bf16[2,32,768]{2,1,0:T(8,128)(2,1)}, bf16[2,32,768]{2,1,0:T(8,128)(2,1)}, u32[]{:S(2)}, u32[]{:S(2)}) collective-permute-start(bf16[2,32,768]{2,1,0:T(8,128)(2,1)} %constant_dynamic-update-slice_fusion), channel_id=1, source_target_pairs={{0,1},{1,0},{2,3},{3,2},{4,5},{5,4},{6,7},{7,6},{8,9},{9,8},{10,11... | collective-permute-start | bytes 294920 | tf_op jit(solution)/shard_map/ppermute | solution.py:39
  60.7 47.3 %copy-start.12 = (bf16[256,768]{0,1:T(8,128)(2,1)S(1)}, bf16[256,768]{0,1:T(8,128)(2,1)}, u32[]{:S(2)}) copy-start(bf16[256,768]{0,1:T(8,128)(2,1)} %copy.156) | copy-start | bytes 1179652
  60.7 47.3 %copy-start.13 = (bf16[256,768]{0,1:T(8,128)(2,1)S(1)}, bf16[256,768]{0,1:T(8,128)(2,1)}, u32[]{:S(2)}) copy-start(bf16[256,768]{0,1:T(8,128)(2,1)} %copy.157) | copy-start | bytes 1179652
  110.4 17.8 %copy-start.41 = (pred[8,12]{1,0:T(8,128)(4,1)S(1)}, pred[8,12]{1,0:T(8,128)(4,1)}, u32[]{:S(2)}) copy-start(pred[8,12]{1,0:T(8,128)(4,1)} %copy-done.40) | copy-start | bytes 292
  112.5 4.4 collective-permute-start.4
  117.8 4.7 collective-permute-start.5
  119.0 6.1 %collective-permute-start.1 = (bf16[2,64,768]{2,1,0:T(8,128)(2,1)S(1)}, bf16[2,64,768]{2,1,0:T(8,128)(2,1)S(1)}, u32[]{:S(2)}, u32[]{:S(2)}) collective-permute-start(bf16[2,64,768]{2,1,0:T(8,128)(2,1)S(1)} %maximum_select_fusion.2), channel_id=1, source_target_pairs={{0,2},{1,3},{2,0},{3,1},{4,6},{5,7},{6,4},{7,5},{8,10},{9,11},{10,... | collective-permute-start | bytes 589832 | tf_op jit(solution)/shard_map/ppermute | solution.py:39
  123.2 17.7 %collective-permute-start.6 = (bf16[8,2,8,768]{3,2,1,0:T(8,128)(2,1)}, bf16[8,2,8,768]{3,2,1,0:T(8,128)(2,1)}, u32[]{:S(2)}, u32[]{:S(2)}) collective-permute-start(bf16[8,2,8,768]{3,2,1,0:T(8,128)(2,1)} %bitcast.18), channel_id=1, source_target_pairs={{0,8},{1,9},{2,10},{3,11},{4,12},{5,13},{6,14},{7,15},{8,0},{9,1},... | collective-permute-start | bytes 589832 | tf_op jit(solution)/shard_map/ppermute | solution.py:25
  125.9 17.0 %collective-permute-start.2 = (bf16[2,128,768]{2,1,0:T(8,128)(2,1)}, bf16[2,128,768]{2,1,0:T(8,128)(2,1)}, u32[]{:S(2)}, u32[]{:S(2)}) collective-permute-start(bf16[2,128,768]{2,1,0:T(8,128)(2,1)} %maximum_select_fusion.1), channel_id=1, source_target_pairs={{0,4},{1,5},{2,6},{3,7},{4,0},{5,1},{6,2},{7,3},{8,12},{9,13},{10,... | collective-permute-start | bytes 1179656 | tf_op jit(solution)/shard_map/ppermute | solution.py:39
  129.6 3.8 copy-start.35
  142.9 16.9 %collective-permute-start.7 = (bf16[16,2,8,768]{3,2,0,1:T(8,128)(2,1)}, bf16[16,2,8,768]{3,2,0,1:T(8,128)(2,1)}, u32[]{:S(2)}, u32[]{:S(2)}) collective-permute-start(bf16[16,2,8,768]{3,2,0,1:T(8,128)(2,1)} %bitcast.21), channel_id=1, source_target_pairs={{0,16},{1,17},{2,18},{3,19},{4,20},{5,21},{6,22},{7,23},{8,24},{9,... | collective-permute-start | bytes 1179656 | tf_op jit(solution)/shard_map/ppermute | solution.py:25
  144.4 4.8 copy-start.37
  162.0 5.0 copy-start.36
  198.4 3.6 copy-start.5
  198.4 3.6 copy-start.11
  198.4 3.6 copy-start.27
  255.8 20.1 %collective-permute-start.8 = (f32[2,128,768]{2,1,0:T(8,128)}, f32[2,128,768]{2,1,0:T(8,128)}, u32[]{:S(2)}, u32[]{:S(2)}) collective-permute-start(f32[2,128,768]{2,1,0:T(8,128)} %broadcast_select_fusion), channel_id=1, source_target_pairs={{0,4},{1,5},{2,6},{3,7},{4,0},{5,1},{6,2},{7,3},{8,12},{9,13},{10,... | collective-permute-start | bytes 2359304 | tf_op jit(solution)/shard_map/ppermute | solution.py:39
  266.3 13.1 %copy-start.9 = (bf16[1,256,768]{1,2,0:T(8,128)(2,1)S(1)}, bf16[1,256,768]{1,2,0:T(8,128)(2,1)}, u32[]{:S(2)}) copy-start(bf16[1,256,768]{1,2,0:T(8,128)(2,1)} %copy.193) | copy-start | bytes 1179652
  266.3 13.1 %copy-start.26 = (f32[12,256,8]{1,2,0:T(8,128)S(1)}, f32[12,256,8]{1,2,0:T(8,128)}, u32[]{:S(2)}) copy-start(f32[12,256,8]{1,2,0:T(8,128)} %fusion.41) | copy-start | bytes 294916
  279.3 21.4 %collective-permute-start.9 = (f32[2,64,768]{2,1,0:T(8,128)}, f32[2,64,768]{2,1,0:T(8,128)}, u32[]{:S(2)}, u32[]{:S(2)}) collective-permute-start(f32[2,64,768]{2,1,0:T(8,128)} %slice_select_fusion), channel_id=1, source_target_pairs={{0,2},{1,3},{2,0},{3,1},{4,6},{5,7},{6,4},{7,5},{8,10},{9,11},{10,... | collective-permute-start | bytes 1179656 | tf_op jit(solution)/shard_map/ppermute | solution.py:39
  297.5 222.2 %reduce-scatter.7.cloned.1.call-start = ((), (), s32[]{:S(2)}) async-start(), calls=%async_computation.3 | async-start | bytes 7299072
  297.6 3.1 copy-start.7
  300.6 3.4 copy-start.3
  302.4 1.6 collective-permute-start.10
  320.0 3.1 copy-start.8
  320.0 3.1 copy-start.30
  320.0 3.1 copy-start.32
  (27 other events, 51.6 us)
Sparse Core Ops, SparseCore 0:
  297.7 96.6 reduce-scatter.4
  401.6 118.1 reduce-scatter.6
